TPU v7x, 32 devices: a whole 2x2x4 slice. The times are simulated.
32 devices in a mesh: group: 2 (over y), tile: 16 (over z, x, core).
Axes of the slice: x: 2, y: 2, z: 4, core: 2. Of those that a mesh axis runs over, the one named last changes fastest.
Arguments:
- vorticity: float32 [16, 1024, 1024], P(None, ('group', 'tile')), may hold values from -6 to 6
- layer_to_mode: float32 [16, 16], replicated, may hold values from -1.5 to 1.5
- mode_to_layer: float32 [16, 16], replicated, may hold values from -1.5 to 1.5
- inverse_radii: float32 [16], replicated, may hold values from 0.001 to 1
- wind_curl: float32 [1024, 1024], P(('group', 'tile')), may hold values from -6 to 6
- wet_mask: int32 [1024, 1024], P(('group', 'tile')), may hold values 0 or 1
Outputs:
- new_vorticity: float32 [16, 1024, 1024], P(None, ('group', 'tile'))
- stream: float32 [16, 1024, 1024], P(None, ('group', 'tile'))
All inputs are finite; a program needn't handle non-finite values. No bound on the sum of `wet_mask` on one device may be relied on, other than what follows from the above.
Results may differ from a plain program's by a relative error of at most 0.00011.
Values sent between devices are 32-bit elements; how exact they have to be, the bound alone decides.
A program may use at most 64 MiB of HBM per device.

v0:
```python
import math

import jax
import jax.numpy as jnp
from jax import lax
from jax.sharding import PartitionSpec as P

time_step = 0.5
beta_plane = 1.0
bottom_drag = 0.2


def extended(cells, sides, width):
    for axis, dim in sides:
        count = lax.axis_size(axis)
        ends = count - 1
        head = lax.slice_in_dim(cells, 0, width, axis=dim)
        tail = lax.slice_in_dim(cells, cells.shape[dim] - width, cells.shape[dim], axis=dim)
        cells = jnp.concatenate(
            [
                lax.ppermute(tail, axis, [(i, (i + 1) % count) for i in range(ends)]),
                cells,
                lax.ppermute(head, axis, [((i + 1) % count, i) for i in range(ends)]),
            ],
            axis=dim,
        )
    return cells


def make_table(length, positions):
    wavenumber = jnp.arange(length, dtype=jnp.int32) + 1
    phase_index = wavenumber[:, None] * (positions[None, :] + 1) % (2 * (length + 1))
    return math.sqrt(2.0 / (length + 1)) * jnp.sin(
        math.pi * phase_index.astype(jnp.float32) / (length + 1)
    )


def eigen_values(length, positions):
    return 4.0 * jnp.sin(math.pi * (positions + 1).astype(jnp.float32) / (2 * (length + 1))) ** 2


def contract(left, right, left_dim, right_dim):
    return lax.dot_general(
        left,
        right,
        (((left_dim,), (right_dim,)), ((), ())),
        precision=lax.Precision.HIGHEST,
        preferred_element_type=jnp.float32,
    )


def offset_view(padded, row_step, column_step):
    height = padded.shape[1] - 2
    breadth = padded.shape[2] - 2
    return padded[
        :, 1 + row_step : 1 + row_step + height, 1 + column_step : 1 + column_step + breadth
    ]


def tendency_of(vortex_pad, stream_pad, wind_curl):
    vortex_north = offset_view(vortex_pad, 1, 0)
    vortex_south = offset_view(vortex_pad, -1, 0)
    vortex_east = offset_view(vortex_pad, 0, 1)
    vortex_west = offset_view(vortex_pad, 0, -1)
    vortex_northeast = offset_view(vortex_pad, 1, 1)
    vortex_northwest = offset_view(vortex_pad, 1, -1)
    vortex_southeast = offset_view(vortex_pad, -1, 1)
    vortex_southwest = offset_view(vortex_pad, -1, -1)
    stream_mid = offset_view(stream_pad, 0, 0)
    stream_north = offset_view(stream_pad, 1, 0)
    stream_south = offset_view(stream_pad, -1, 0)
    stream_east = offset_view(stream_pad, 0, 1)
    stream_west = offset_view(stream_pad, 0, -1)
    stream_northeast = offset_view(stream_pad, 1, 1)
    stream_northwest = offset_view(stream_pad, 1, -1)
    stream_southeast = offset_view(stream_pad, -1, 1)
    stream_southwest = offset_view(stream_pad, -1, -1)
    arakawa_one = (stream_east - stream_west) * (vortex_north - vortex_south) - (
        stream_north - stream_south
    ) * (vortex_east - vortex_west)
    arakawa_two = (
        stream_east * (vortex_northeast - vortex_southeast)
        - stream_west * (vortex_northwest - vortex_southwest)
        - stream_north * (vortex_northeast - vortex_northwest)
        + stream_south * (vortex_southeast - vortex_southwest)
    )
    arakawa_three = (
        vortex_north * (stream_northeast - stream_northwest)
        - vortex_south * (stream_southeast - stream_southwest)
        - vortex_east * (stream_northeast - stream_southeast)
        + vortex_west * (stream_northwest - stream_southwest)
    )
    jacobian = (arakawa_one + arakawa_two + arakawa_three) / 12.0
    laplace = stream_north + stream_south + stream_east + stream_west - 4.0 * stream_mid
    layers = stream_mid.shape[0]
    layer_index = jnp.arange(layers, dtype=jnp.int32)
    top_layer = (layer_index == 0).astype(jnp.float32)[:, None, None]
    bottom_layer = (layer_index == layers - 1).astype(jnp.float32)[:, None, None]
    return (
        -jacobian
        - beta_plane * 0.5 * (stream_east - stream_west)
        + top_layer * wind_curl[None]
        - bottom_drag * bottom_layer * laplace
    )


def body(vorticity, layer_to_mode, mode_to_layer, inverse_radii, wind_curl, wet_mask):
    grid_width = vorticity.shape[2]
    natural = jnp.arange(grid_width, dtype=jnp.int32)
    sine = make_table(grid_width, natural)
    row_eigen = eigen_values(grid_width, natural)
    tile_count = lax.axis_size("tile")
    vortex_ext = extended(vorticity, ((("group", "tile"), 1),), 1)
    modal_field = contract(layer_to_mode, vorticity, 1, 0)
    column_spectrum = contract(modal_field, sine, 2, 0)
    spread = lax.all_to_all(
        column_spectrum, ("group", "tile"), split_axis=2, concat_axis=1, tiled=True
    )
    wave_count = spread.shape[2]
    first_wave = (lax.axis_index("group") * tile_count + lax.axis_index("tile")) * wave_count
    column_eigen = eigen_values(grid_width, first_wave + jnp.arange(wave_count, dtype=jnp.int32))
    spectrum = contract(spread, sine, 1, 0)
    stream_spectrum = -spectrum / (
        row_eigen[None, None, :] + column_eigen[None, :, None] + inverse_radii[:, None, None]
    )
    stream_rows = contract(stream_spectrum, sine, 2, 0)
    stream_columns = lax.all_to_all(
        stream_rows, ("group", "tile"), split_axis=2, concat_axis=1, tiled=True
    )
    stream_modes = contract(stream_columns, sine, 1, 0)
    stream = contract(mode_to_layer, stream_modes, 1, 0)
    stream_ext = extended(stream, ((("group", "tile"), 1),), 1)
    padding = ((0, 0), (0, 0), (1, 1))
    tendency = tendency_of(jnp.pad(vortex_ext, padding), jnp.pad(stream_ext, padding), wind_curl)
    return (vorticity + time_step * wet_mask.astype(jnp.float32) * tendency, stream)


def solution(mesh):
    return jax.shard_map(
        body,
        mesh=mesh,
        in_specs=(
            P(None, ("group", "tile"), None),
            P(),
            P(),
            P(),
            P(("group", "tile"), None),
            P(("group", "tile"), None),
        ),
        out_specs=(P(None, ("group", "tile"), None), P(None, ("group", "tile"), None)),
        check_vma=False,
    )
```

profile of v0, /device:TPU:4, one launch (start us, length us, event | category | flops | bytes accessed | tf_op | source)
XLA Modules:
  0.0 331.6 jit_solution(383074206940932705)
XLA Ops:
  1.3 4.4 %fusion.53 = f32[16,32,1024]{2,0,1:T(8,128)S(1)} fusion(f32[16,16]{1,0:T(8,128)S(1)} %copy-done, f32[16,32,1024]{2,1,0:T(8,128)} %param.6), kind=kOutput, calls=%fused_computation.67 | convolution fusion | flops 100663296 | bytes 4195328 | tf_op jit(solution)/shard_map/dot_general | solution.py:43
  5.7 23.6 %fusion.14 = f32[16,32,1024]{2,0,1:T(8,128)S(1)} fusion(f32[16,32,1024]{2,0,1:T(8,128)S(1)} %fusion.53, s32[1024]{0:T(1024)S(1)} %iota_add_fusion), kind=kOutput, calls=%fused_computation.15 | convolution fusion | flops 6452936704 | bytes 4198400 | tf_op jit(solution)/shard_map/dot_general | solution.py:43
  29.3 6.5 %copy.28 = f32[16,32,1024]{1,0,2:T(8,128)} copy(f32[16,32,1024]{2,0,1:T(8,128)S(1)} %fusion.14) | data formatting | bytes 4194304 | tf_op jit(solution)/shard_map/dot_general | solution.py:43
  35.8 7.7 %reshape.81 = f32[32,1,16384]{2,1,0:T(1,128)} reshape(f32[1024,16,32]{2,1,0:T(8,128)} %bitcast.37) | data formatting | bytes 4194304
  43.6 6.7 %all-to-all-start = ((f32[32,1,16384]{2,1,0:T(1,128)}), f32[32,1,16384]{2,1,0:T(1,128)S(1)}, u32[]{:S(2)}, u32[]{:S(2)}) async-start(f32[32,1,16384]{2,1,0:T(1,128)} %reshape.81), calls=%async_computation | async-start | bytes 4194304 | tf_op jit(solution)/shard_map/all_to_all | solution.py:116
  50.5 48.6 %all-to-all-done = f32[32,1,16384]{2,1,0:T(1,128)S(1)} async-done(((f32[32,1,16384]{2,1,0:T(1,128)}), f32[32,1,16384]{2,1,0:T(1,128)S(1)}, u32[]{:S(2)}, u32[]{:S(2)}) %all-to-all-start) | async-done | bytes 2097184 | tf_op jit(solution)/shard_map/all_to_all | solution.py:116
  100.9 7.7 %reduce = f32[32,16384]{1,0:T(8,128)S(1)} reduce(f32[32,1,16384]{2,1,0:T(1,128)} %copy-done.2, f32[]{:T(128)} %broadcast.144), dimensions={1}, to_apply=%all_to_all.26.reduce_sub_computation | reduce | bytes 4194308 | tf_op jit(solution)/shard_map/all_to_all | solution.py:116
  108.5 4.8 %reshape.82 = f32[1024,16,32]{2,1,0:T(8,128)} reshape(f32[32,16384]{1,0:T(8,128)S(1)} %reduce) | data formatting | bytes 4194304
  113.3 11.5 %copy.51 = f32[16,32,32,32]{1,2,3,0:T(8,128)} copy(f32[16,32,32,32]{1,0,3,2:T(8,128)} %bitcast.39) | data formatting | bytes 4194304 | tf_op jit(solution)/shard_map/all_to_all | solution.py:116
  124.8 6.6 %all_to_all.29 = f32[16,1024,32]{1,2,0:T(8,128)S(1)} reshape(f32[16,32,32,32]{2,1,3,0:T(8,128)} %bitcast.40) | data formatting | bytes 4194304 | tf_op jit(solution)/shard_map/all_to_all | solution.py:116
  131.4 23.6 %fusion.12 = f32[16,32,1024]{2,1,0:T(8,128)S(1)} fusion(f32[16,1024,32]{1,2,0:T(8,128)S(1)} %all_to_all.29, s32[1024]{0:T(1024)S(1)} %iota_add_fusion), kind=kOutput, calls=%fused_computation.14 | convolution fusion | flops 6452936704 | bytes 4198400 | tf_op jit(solution)/shard_map/dot_general | solution.py:43
  155.0 24.3 %fusion.10 = f32[16,32,1024]{2,1,0:T(8,128)S(1)} fusion(f32[16,32,1024]{2,1,0:T(8,128)S(1)} %fusion.12, s32[1024]{0:T(1024)S(1)} %iota_add_fusion, f32[16]{0:T(128)S(1)} %copy-done.6, f32[32,1024]{1,0:T(8,128)S(1)} %broadcast_add_fusion), kind=kOutput, calls=%fused_computation.13 | convolution fusion | flops 6454509568 | bytes 4329536 | tf_op jit(solution)/shard_map/dot_general | solution.py:43
  179.3 6.4 %copy.30 = f32[16,32,1024]{1,0,2:T(8,128)} copy(f32[16,32,1024]{2,1,0:T(8,128)S(1)} %fusion.10) | data formatting | bytes 4194304 | tf_op jit(solution)/shard_map/dot_general | solution.py:43
  185.7 7.7 %reshape.83 = f32[32,1,16384]{2,1,0:T(1,128)} reshape(f32[1024,16,32]{2,1,0:T(8,128)} %bitcast.38) | data formatting | bytes 4194304
  193.4 4.1 %all-to-all-start.1 = ((f32[32,1,16384]{2,1,0:T(1,128)}), f32[32,1,16384]{2,1,0:T(1,128)}, u32[]{:S(2)}, u32[]{:S(2)}) async-start(f32[32,1,16384]{2,1,0:T(1,128)} %reshape.83), calls=%async_computation.1 | async-start | bytes 4194304 | tf_op jit(solution)/shard_map/all_to_all | solution.py:127
  200.4 6.0 %collective-permute-start.2 = (f32[16,1,1024]{2,0,1:T(8,128)S(1)}, f32[16,1,1024]{2,0,1:T(8,128)S(1)}, u32[]{:S(2)}, u32[]{:S(2)}) collective-permute-start(f32[16,1,1024]{2,0,1:T(8,128)S(1)} %get-tuple-element.9), channel_id=1, source_target_pairs={{1,0},{2,1},{3,2},{4,3},{5,4},{6,5},{7,6},{8,7},{9,8},{10,9},{11,1... | collective-permute-start | bytes 196616 | tf_op jit(solution)/shard_map/ppermute | solution.py:23
  208.4 38.2 %all-to-all-done.1 = f32[32,1,16384]{2,1,0:T(1,128)} async-done(((f32[32,1,16384]{2,1,0:T(1,128)}), f32[32,1,16384]{2,1,0:T(1,128)}, u32[]{:S(2)}, u32[]{:S(2)}) %all-to-all-start.1) | async-done | bytes 2097184 | tf_op jit(solution)/shard_map/all_to_all | solution.py:127
  246.6 8.7 %reduce.1 = f32[32,16384]{1,0:T(8,128)} reduce(f32[32,1,16384]{2,1,0:T(1,128)} %all-to-all-done.1, f32[]{:T(128)} %broadcast.144), dimensions={1}, to_apply=%all_to_all.30.reduce_sub_computation | reduce | bytes 4194308 | tf_op jit(solution)/shard_map/all_to_all | solution.py:127
  255.3 6.4 %reshape.84 = f32[1024,16,32]{2,1,0:T(8,128)} reshape(f32[32,16384]{1,0:T(8,128)} %reduce.1) | data formatting | bytes 4194304
  261.7 11.5 %copy.50 = f32[16,32,32,32]{1,2,3,0:T(8,128)} copy(f32[16,32,32,32]{1,0,3,2:T(8,128)} %bitcast.41) | data formatting | bytes 4194304 | tf_op jit(solution)/shard_map/all_to_all | solution.py:127
  273.2 7.7 %all_to_all.33 = f32[16,1024,32]{1,2,0:T(8,128)} reshape(f32[16,32,32,32]{2,1,3,0:T(8,128)} %bitcast.42) | data formatting | bytes 4194304 | tf_op jit(solution)/shard_map/all_to_all | solution.py:127
  280.9 26.9 %fusion.8 = f32[16,32,1024]{2,0,1:T(8,128)S(1)} fusion(f32[16,1024,32]{1,2,0:T(8,128)} %all_to_all.33, s32[1024]{0:T(1024)S(1)} %iota_add_fusion), kind=kOutput, calls=%fused_computation.12 | convolution fusion | flops 6452936704 | bytes 4198400 | tf_op jit(solution)/shard_map/dot_general | solution.py:43
  311.9 7.2 %collective-permute-start.1 = (f32[16,1,1024]{2,0,1:T(8,128)S(1)}, f32[16,1,1024]{2,0,1:T(8,128)S(1)}, u32[]{:S(2)}, u32[]{:S(2)}) collective-permute-start(f32[16,1,1024]{2,0,1:T(8,128)S(1)} %get-tuple-element.11), channel_id=1, source_target_pairs={{1,0},{2,1},{3,2},{4,3},{5,4},{6,5},{7,6},{8,7},{9,8},{10,9},{11,1... | collective-permute-start | bytes 196616 | tf_op jit(solution)/shard_map/ppermute | solution.py:23
  323.3 5.3 %multiply_add_fusion = f32[16,32,1024]{2,0,1:T(8,128)S(1)} fusion(f32[16,32,1024]{2,0,1:T(8,128)S(1)} %copy.38, f32[16,32,1024]{2,0,1:T(8,128)S(1)} %convolution_bitcast_fusion, f32[16,34,1026]{2,0,1:T(8,128)S(1)} %select_maximum_fusion.2, f32[16,1,1024]{2,0,1:T(8,128)S(1)} %collective-permute-done, f32[16,1,1024]{2,0,1:T(8,128)S(1)} %collective-permute-done.1, ...), kind=kLoop, calls=%fused_computation.28 | loop fusion | flops 26214400 | bytes 31981696 | tf_op jit(solution)/shard_map/add | solution.py:135
  (36 shorter events, 18.2 us)
Async XLA Ops:
  0.6 0.7 copy-start
  43.6 55.5 %all-to-all-start = ((f32[32,1,16384]{2,1,0:T(1,128)}), f32[32,1,16384]{2,1,0:T(1,128)S(1)}, u32[]{:S(2)}, u32[]{:S(2)}) async-start(f32[32,1,16384]{2,1,0:T(1,128)} %reshape.81), calls=%async_computation | async-start | bytes 4194304 | tf_op jit(solution)/shard_map/all_to_all | solution.py:116
  99.0 1.3 copy-start.2
  131.4 23.6 %copy-start.6 = (f32[16]{0:T(128)S(1)}, f32[16]{0:T(128)}, u32[]{:S(2)}) copy-start(f32[16]{0:T(128)} %param.9) | copy-start | bytes 196
  193.4 53.2 %all-to-all-start.1 = ((f32[32,1,16384]{2,1,0:T(1,128)}), f32[32,1,16384]{2,1,0:T(1,128)}, u32[]{:S(2)}, u32[]{:S(2)}) async-start(f32[32,1,16384]{2,1,0:T(1,128)} %reshape.83), calls=%async_computation.1 | async-start | bytes 4194304 | tf_op jit(solution)/shard_map/all_to_all | solution.py:127
  197.5 10.8 %copy-start.4 = (s32[32,1024]{1,0:T(8,128)S(1)}, s32[32,1024]{1,0:T(8,128)}, u32[]{:S(2)}) copy-start(s32[32,1024]{1,0:T(8,128)} %param.11) | copy-start | bytes 393220
  200.4 118.7 %collective-permute-start.2 = (f32[16,1,1024]{2,0,1:T(8,128)S(1)}, f32[16,1,1024]{2,0,1:T(8,128)S(1)}, u32[]{:S(2)}, u32[]{:S(2)}) collective-permute-start(f32[16,1,1024]{2,0,1:T(8,128)S(1)} %get-tuple-element.9), channel_id=1, source_target_pairs={{1,0},{2,1},{3,2},{4,3},{5,4},{6,5},{7,6},{8,7},{9,8},{10,9},{11,1... | collective-permute-start | bytes 196616 | tf_op jit(solution)/shard_map/ppermute | solution.py:23
  206.4 112.7 %collective-permute-start.3 = (f32[16,1,1024]{2,0,1:T(8,128)S(1)}, f32[16,1,1024]{2,0,1:T(8,128)S(1)}, u32[]{:S(2)}, u32[]{:S(2)}) collective-permute-start(f32[16,1,1024]{2,0,1:T(8,128)S(1)} %get-tuple-element.8), channel_id=1, source_target_pairs={{0,1},{1,2},{2,3},{3,4},{4,5},{5,6},{6,7},{7,8},{8,9},{9,10},{10,1... | collective-permute-start | bytes 196616 | tf_op jit(solution)/shard_map/ppermute | solution.py:21
  280.9 27.0 %copy-start.5 = (f32[16,16]{1,0:T(8,128)S(1)}, f32[16,16]{1,0:T(8,128)}, u32[]{:S(2)}) copy-start(f32[16,16]{1,0:T(8,128)} %param.8) | copy-start | bytes 3076
  310.0 12.5 %collective-permute-start = (f32[16,1,1024]{2,0,1:T(8,128)S(1)}, f32[16,1,1024]{2,0,1:T(8,128)S(1)}, u32[]{:S(2)}, u32[]{:S(2)}) collective-permute-start(f32[16,1,1024]{2,0,1:T(8,128)S(1)} %get-tuple-element.10), channel_id=1, source_target_pairs={{0,1},{1,2},{2,3},{3,4},{4,5},{5,6},{6,7},{7,8},{8,9},{9,10},{10,1... | collective-permute-start | bytes 196616 | tf_op jit(solution)/shard_map/ppermute | solution.py:21
  311.9 10.5 %collective-permute-start.1 = (f32[16,1,1024]{2,0,1:T(8,128)S(1)}, f32[16,1,1024]{2,0,1:T(8,128)S(1)}, u32[]{:S(2)}, u32[]{:S(2)}) collective-permute-start(f32[16,1,1024]{2,0,1:T(8,128)S(1)} %get-tuple-element.11), channel_id=1, source_target_pairs={{1,0},{2,1},{3,2},{4,3},{5,4},{6,5},{7,6},{8,7},{9,8},{10,9},{11,1... | collective-permute-start | bytes 196616 | tf_op jit(solution)/shard_map/ppermute | solution.py:23
  322.4 0.9 copy-start.3
  323.3 7.8 %copy-start.1 = (f32[16,16]{1,0:T(8,128)S(1)}, f32[16,16]{1,0:T(8,128)}, u32[]{:S(2)}) copy-start(f32[16,16]{1,0:T(8,128)} %param.7) | copy-start | bytes 3076
where the time goes:
time: 335 us; the launch traced here: 332 us
  matrix products  105 us (31%)
  local copies, waits for them, and re-layouts  87.5 us (26%)
  waiting for transfers between devices  86.8 us (26%)
  starting transfers between devices  27.8 us (8%)
  other arithmetic  23.3 us (7%)
    dot_general x6, matrix products, contract(): lax.dot_general(left, right, (((left_dim,), (right_dim,)), ((), ())), pre...  105 us
    all_to_all x1, waiting for transfers between devices, body(): lax.all_to_all(column_spectrum, ('group', 'tile'), split_axis=2, concat_a...  48.6 us
    all_to_all x1, waiting for transfers between devices, body(): lax.all_to_all(stream_rows, ('group', 'tile'), split_axis=2, concat_axis=...  38.2 us
    unnamed x21, local copies, waits for them, and re-layouts  36.8 us
    all_to_all x2, local copies, waits for them, and re-layouts, body(): lax.all_to_all(stream_rows, ('group', 'tile'), split_axis=2, concat_axis=...  19.2 us
    all_to_all x3, local copies, waits for them, and re-layouts, body(): lax.all_to_all(column_spectrum, ('group', 'tile'), split_axis=2, concat_a...  18.6 us
    ppermute x2, starting transfers between devices, extended(): lax.ppermute(head, axis, [((i + 1) % count, i) for i in range(ends)])  13.2 us
    dot_general x2, local copies, waits for them, and re-layouts, contract(): lax.dot_general(left, right, (((left_dim,), (right_dim,)), ((), ())), pre...  12.9 us
  transfers between devices with their start and end apart: 6, of which 2 were waited for; matrix products, arithmetic and copies ran while one was open for 19% of the time, Pallas kernels for 0%

commit v1 on v0

v1 whole, which is shorter than its diff:
```python
import functools
import math

import jax
import jax.numpy as jnp
import ml_dtypes
import numpy as np
from jax import lax
from jax.experimental import pallas as pl
from jax.experimental.pallas import tpu as pltpu
from jax.sharding import PartitionSpec as P

time_step = 0.5
beta_plane = 1.0
bottom_drag = 0.2
MESH = pl.DeviceIdType.MESH
VMEM = pl.BlockSpec(memory_space=pltpu.VMEM)
SMEM = pl.BlockSpec(memory_space=pltpu.SMEM)


def sine_parts(length):
    wave = np.arange(length, dtype=np.int64) + 1
    phase = (wave[:, None] * wave[None, :]) % (2 * (length + 1))
    table = math.sqrt(2.0 / (length + 1)) * np.sin(math.pi * phase / (length + 1))
    high = table.astype(np.float32).astype(ml_dtypes.bfloat16)
    low = (table - high.astype(np.float64)).astype(np.float32).astype(ml_dtypes.bfloat16)
    return high, low


def eigen_values(length):
    wave = np.arange(length, dtype=np.float64) + 1
    return (4.0 * np.sin(math.pi * wave / (2 * (length + 1))) ** 2).astype(np.float32)


def halves(value):
    high = value.astype(jnp.bfloat16)
    low = (value - high.astype(jnp.float32)).astype(jnp.bfloat16)
    return high, low


def dot(left, right):
    return jnp.dot(left, right, preferred_element_type=jnp.float32)


def dot3(left, right):
    (left_high, left_low), (right_high, right_low) = left, right
    return dot(left_high, right_high) + (dot(left_low, right_high) + dot(left_high, right_low))


def power(base, exponent):
    result = None
    while exponent:
        if exponent & 1:
            result = base if result is None else result * base
        exponent >>= 1
        if exponent:
            base = base * base
    return result


def roots(shift):
    width = jnp.sqrt(shift + 0.25 * shift * shift)
    inverse = 1.0 + 0.5 * shift + width
    return 1.0 / inverse, inverse, width


def radius_column(radii, layers):
    position = lax.broadcasted_iota(jnp.int32, (layers, 1), 0)
    column = jnp.zeros((layers, 1), jnp.float32)
    for mode in range(layers):
        column = jnp.where(position == mode, radii[mode], column)
    return column


def spread_matrix(matrix, count, gather):
    size = matrix.shape[0]
    whole = size * count
    row = lax.broadcasted_iota(jnp.int32, (whole, size), 0)
    item = lax.broadcasted_iota(jnp.int32, (whole, size), 1)
    row_item = row % size if gather else row // count
    left = (row_item == item).astype(jnp.bfloat16)
    column = lax.broadcasted_iota(jnp.int32, (size, whole), 1)
    item = lax.broadcasted_iota(jnp.int32, (size, whole), 0)
    column_item = column // count if gather else column % size
    right = (column_item == item).astype(jnp.bfloat16)
    row = lax.broadcasted_iota(jnp.int32, (whole, whole), 0)
    column = lax.broadcasted_iota(jnp.int32, (whole, whole), 1)
    if gather:
        same = row // size == column % count
    else:
        same = row % count == column // size
    parts = []
    for part in halves(matrix):
        full = dot(dot(left, part).astype(jnp.bfloat16), right)
        parts.append(jnp.where(same, full, 0.0).astype(jnp.bfloat16))
    return tuple(parts)


def forward_kernel(
    sizes, vortex, to_mode, radii, eigen, sine_high, sine_low,
    field, carried, vortex_edge,
    edge, moments, gathered, solved, landed, edge_landed,
    send_a, recv_a, send_b, recv_b, send_e, recv_e,
):
    groups, tiles, layers, rows, width, piece = sizes
    count = groups * tiles
    per_mode = width // piece
    me = lax.axis_index("group") * tiles + lax.axis_index("tile")

    def place(index):
        return (index // tiles, index % tiles)

    barrier = pltpu.get_barrier_semaphore()

    @pl.loop(1, count)
    def _(step):
        pl.semaphore_signal(
            barrier, inc=1, device_id=place((me + step) % count), device_id_type=MESH
        )

    edge[0] = vortex[:, rows - 1, :]
    edge[1] = vortex[:, 0, :]
    pl.semaphore_wait(barrier, count - 1)

    def edge_copy(side):
        target = (me + 1) % count if side == 0 else (me + count - 1) % count
        return pltpu.make_async_remote_copy(
            src_ref=edge.at[side], dst_ref=edge_landed.at[side],
            send_sem=send_e.at[side], recv_sem=recv_e.at[side],
            device_id=place(target), device_id_type=MESH,
        )

    edge_copy(0).start()
    edge_copy(1).start()

    chunk = min(rows, 16)
    mixer = spread_matrix(to_mode[...], chunk, True)
    shift = radius_column(radii, layers) + eigen[...]
    rho, _, _ = roots(shift)
    for part in range(rows // chunk):
        block = vortex[:, part * chunk : (part + 1) * chunk, :].reshape(layers * chunk, width)
        modal = halves(dot3(mixer, halves(block)))
        spectrum = dot3(modal, (sine_high[...], sine_low[...]))
        field[part * chunk : (part + 1) * chunk] = spectrum.reshape(chunk, layers, width)

    ahead = field[0]
    for y in range(1, rows):
        ahead = ahead * rho + field[y]
    behind = field[rows - 1] * rho
    for y in range(rows - 2, -1, -1):
        behind = (behind + field[y]) * rho
    for mode in range(layers):
        for part in range(per_mode):
            span = slice(part * piece, (part + 1) * piece)
            moments[mode * per_mode + part, 0:1, :] = ahead[mode : mode + 1, span]
            moments[mode * per_mode + part, 1:2, :] = behind[mode : mode + 1, span]

    def exchange(source, target, send, recv, step):
        other = (me + step) % count
        return pltpu.make_async_remote_copy(
            src_ref=source.at[other], dst_ref=target.at[me],
            send_sem=send.at[step], recv_sem=recv.at[step],
            device_id=place(other), device_id_type=MESH,
        )

    @pl.loop(1, count)
    def _(step):
        exchange(moments, gathered, send_a, recv_a, step).start()

    gathered[me] = moments[me]
    mine = eigen[0:1, 0:piece]
    for part in range(1, per_mode):
        mine = jnp.where(me % per_mode == part, eigen[0:1, part * piece : (part + 1) * piece], mine)
    own, _, _ = roots(mine + radii[me // per_mode])
    stride = power(own, rows)
    whole = power(own, count * rows + 1)
    scale = 1.0 / (1.0 - whole * whole)

    @pl.loop(1, count)
    def _(step):
        exchange(moments, gathered, send_a, recv_a, step).wait_recv()

    total_ahead = gathered[0, 0:1, :]
    for p in range(1, count):
        total_ahead = total_ahead * stride + gathered[p, 0:1, :]
    total_ahead = total_ahead * own
    total_behind = gathered[count - 1, 1:2, :]
    for p in range(count - 2, -1, -1):
        total_behind = total_behind * stride + gathered[p, 1:2, :]
    first = (total_ahead * whole - total_behind) * scale
    last = (total_behind * whole - total_ahead) * scale * own
    for p in range(count):
        solved[p, 0:1, :] = first
        first = first * stride + gathered[p, 0:1, :]
    for p in range(count - 1, -1, -1):
        solved[p, 1:2, :] = last
        last = last * stride + gathered[p, 1:2, :]

    @pl.loop(1, count)
    def _(step):
        exchange(solved, landed, send_b, recv_b, step).start()

    landed[me] = solved[me]
    edge_copy(0).wait()
    edge_copy(1).wait()
    vortex_edge[0] = jnp.where(me == 0, 0.0, edge_landed[0])
    vortex_edge[1] = jnp.where(me == count - 1, 0.0, edge_landed[1])

    @pl.loop(1, count)
    def _(step):
        exchange(solved, landed, send_b, recv_b, step).wait_recv()

    for mode in range(layers):
        for part in range(per_mode):
            span = slice(part * piece, (part + 1) * piece)
            carried[0, mode : mode + 1, span] = landed[mode * per_mode + part, 0:1, :]
            carried[1, mode : mode + 1, span] = landed[mode * per_mode + part, 1:2, :]

    @pl.loop(1, count)
    def _(step):
        exchange(moments, gathered, send_a, recv_a, step).wait_send()
        exchange(solved, landed, send_b, recv_b, step).wait_send()


def backward_kernel(
    sizes, field, carried, vortex_edge, vortex, wind, mask, to_layer, radii, eigen,
    sine_high, sine_low,
    fresh, stream,
    high, low, stream_pad, vortex_pad, turn, cross,
):
    groups, tiles, layers, rows, width, piece = sizes
    count = groups * tiles
    me = lax.axis_index("group") * tiles + lax.axis_index("tile")
    shift = radius_column(radii, layers) + eigen[...]
    rho, inverse, spread = roots(shift)
    factor = -0.5 / spread

    def keep(slot, value):
        upper, lower = halves(value * factor)
        high[slot * layers : (slot + 1) * layers, :] = upper
        low[slot * layers : (slot + 1) * layers, :] = lower

    ahead = carried[0]
    for y in range(rows):
        ahead = ahead * rho + field[y]
        turn[y] = ahead
    behind = carried[1]
    keep(rows + 1, jnp.where(me == count - 1, 0.0, ahead * rho + behind * inverse))
    for y in range(rows - 1, -1, -1):
        keep(y, turn[y] + behind)
        behind = (behind + field[y]) * rho
    keep(rows, jnp.where(me == 0, 0.0, carried[0] + behind))

    chunk = min(rows, 16)
    top = 8
    sine = (sine_high[...], sine_low[...])
    mixer = spread_matrix(to_layer[...], chunk, False)
    for part in range(rows // chunk):
        span = slice(part * chunk * layers, (part + 1) * chunk * layers)
        modes = dot3((high[span, :], low[span, :]), sine)
        mixed = dot3(mixer, halves(modes)).reshape(layers, chunk, width)
        stream[:, part * chunk : (part + 1) * chunk, :] = mixed
        stream_pad[:, top + part * chunk : top + (part + 1) * chunk, :] = mixed
    span = slice(rows * layers, (rows + 2) * layers)
    modes = dot3((high[span, :], low[span, :]), sine)
    plain = halves(to_layer[...])
    stream_pad[:, top - 1, :] = dot3(plain, halves(modes[:layers]))
    stream_pad[:, top + rows, :] = dot3(plain, halves(modes[layers:]))
    vortex_pad[:, top : top + rows, :] = vortex[...]
    vortex_pad[:, top - 1, :] = vortex_edge[0]
    vortex_pad[:, top + rows, :] = vortex_edge[1]

    deep = rows + 2 * top
    lane = lax.broadcasted_iota(jnp.int32, (deep, width), 1)

    def east_west(value):
        lanes = lane[: value.shape[0]]
        east = jnp.where(lanes == width - 1, 0.0, pltpu.roll(value, width - 1, 1))
        west = jnp.where(lanes == 0, 0.0, pltpu.roll(value, 1, 1))
        return east, west

    middle = slice(top, top + rows)
    north = slice(top + 1, top + rows + 1)
    south = slice(top - 1, top + rows - 1)
    damp = mask[...].astype(jnp.float32) * time_step

    @pl.loop(0, layers)
    def _(layer):
        s_all = stream_pad[layer]
        q_all = vortex_pad[layer]
        s_east, s_west = east_west(s_all)
        q_east, q_west = east_west(q_all)
        s_across = s_east - s_west
        q_across = q_east - q_west
        cross[...] = q_all * s_across - s_all * q_across
        s_mid, q_mid = s_all[middle], q_all[middle]
        s_north, s_south = stream_pad[layer, north, :], stream_pad[layer, south, :]
        s_up = s_north - s_south
        q_up = vortex_pad[layer, north, :] - vortex_pad[layer, south, :]
        p_east, p_west = east_west(s_mid * q_up - q_mid * s_up)
        across = s_across[middle]
        jacobian = (
            across * q_up
            - s_up * q_across[middle]
            + (p_east - p_west)
            + (cross[north, :] - cross[south, :])
        ) * (1.0 / 12.0)
        tendency = -jacobian - (beta_plane * 0.5) * across
        forcing = jnp.where(layer == 0, wind[...], 0.0)
        laplace = s_north + s_south + s_east[middle] + s_west[middle] - 4.0 * s_mid
        drag = jnp.where(layer == layers - 1, bottom_drag, 0.0)
        fresh[layer] = q_mid + damp * (tendency + forcing - drag * laplace)


def body(groups, tiles, vorticity, layer_to_mode, mode_to_layer, inverse_radii, wind, mask):
    layers, rows, width = vorticity.shape
    count = groups * tiles
    piece = layers * width // count
    sizes = (groups, tiles, layers, rows, width, piece)
    sine_high, sine_low = (jnp.asarray(part) for part in sine_parts(width))
    eigen = jnp.asarray(eigen_values(width)[None])
    limit = 56 * 1024 * 1024
    f32, bf16 = jnp.float32, jnp.bfloat16
    dma = pltpu.SemaphoreType.DMA
    field, carried, vortex_edge = pl.pallas_call(
        functools.partial(forward_kernel, sizes),
        out_shape=(
            jax.ShapeDtypeStruct((rows, layers, width), f32),
            jax.ShapeDtypeStruct((2, layers, width), f32),
            jax.ShapeDtypeStruct((2, layers, width), f32),
        ),
        in_specs=[VMEM, VMEM, SMEM, VMEM, VMEM, VMEM],
        out_specs=(VMEM, VMEM, VMEM),
        scratch_shapes=[
            pltpu.VMEM((2, layers, width), f32),
            pltpu.VMEM((count, 2, piece), f32),
            pltpu.VMEM((count, 2, piece), f32),
            pltpu.VMEM((count, 2, piece), f32),
            pltpu.VMEM((count, 2, piece), f32),
            pltpu.VMEM((2, layers, width), f32),
            dma((count,)), dma((count,)), dma((count,)), dma((count,)), dma((2,)), dma((2,)),
        ],
        compiler_params=pltpu.CompilerParams(
            collective_id=0, has_side_effects=True, vmem_limit_bytes=limit
        ),
        name="forward",
    )(vorticity, layer_to_mode, inverse_radii, eigen, sine_high, sine_low)
    total = (rows + 2) * layers
    return pl.pallas_call(
        functools.partial(backward_kernel, sizes),
        out_shape=(
            jax.ShapeDtypeStruct((layers, rows, width), f32),
            jax.ShapeDtypeStruct((layers, rows, width), f32),
        ),
        in_specs=[VMEM] * 7 + [SMEM] + [VMEM] * 3,
        out_specs=(VMEM, VMEM),
        scratch_shapes=[
            pltpu.VMEM((total, width), bf16),
            pltpu.VMEM((total, width), bf16),
            pltpu.VMEM((layers, rows + 16, width), f32),
            pltpu.VMEM((layers, rows + 16, width), f32),
            pltpu.VMEM((rows, layers, width), f32),
            pltpu.VMEM((rows + 16, width), f32),
        ],
        compiler_params=pltpu.CompilerParams(vmem_limit_bytes=limit),
        name="backward",
    )(
        field, carried, vortex_edge, vorticity, wind, mask, mode_to_layer, inverse_radii,
        eigen, sine_high, sine_low,
    )


def solution(mesh):
    groups, tiles = mesh.shape["group"], mesh.shape["tile"]
    rows = P(None, ("group", "tile"), None)
    plane = P(("group", "tile"), None)
    return jax.shard_map(
        functools.partial(body, groups, tiles),
        mesh=mesh,
        in_specs=(rows, P(), P(), P(), plane, plane),
        out_specs=(rows, rows),
        check_vma=False,
    )
```

time: 335 us -> 47 us (0.14)
  the two profiles are of different devices: /device:TPU:4 before, /device:TPU:0 now
where the time goes in v1:
time: 47 us; the launch traced here: 46.9 us
  Pallas kernels  46.3 us (99%)
  between operations  0.64 us (1%)
    pallas_call x1, Pallas kernels, body(): pl.pallas_call(functools.partial(forward_kernel, sizes), out_shape=(jax.S...  28.4 us
    pallas_call x1, Pallas kernels, body(): pl.pallas_call(functools.partial(backward_kernel, sizes), out_shape=(jax....  17.9 us

profile of v1, /device:TPU:0, one launch (start us, length us, event | category | flops | bytes accessed | tf_op | source)
XLA Modules:
  0.0 46.9 jit_solution(3133237227810572740)
XLA Ops:
  0.6 28.4 %forward.1 = (f32[32,16,1024]{2,1,0:T(8,128)}, f32[2,16,1024]{2,1,0:T(8,128)}, f32[2,16,1024]{2,1,0:T(8,128)}) custom-call(f32[16,32,1024]{2,1,0:T(8,128)} %vortex.3, f32[16,16]{1,0:T(8,128)} %to_mode.1, f32[16]{0:T(128)} %radii.3, f32[1,1024]{1,0:T(1,128)} %constant.8.clone.eigen, bf16[1024,1024]{1,0:T(8,128)(2,1)} %constant.6.clone.sine_high, ...), custom_call_target="tpu_custom_call" | custom-call | tf_op jit(solution)/shard_map/forward/pallas_call | solution.py:325
  29.0 17.9 %backward.1 = (f32[16,32,1024]{2,1,0:T(8,128)}, f32[16,32,1024]{2,1,0:T(8,128)}) custom-call(f32[32,16,1024]{2,1,0:T(8,128)} %get-tuple-element.5.field, f32[2,16,1024]{2,1,0:T(8,128)} %get-tuple-element.6.carried, f32[2,16,1024]{2,1,0:T(8,128)} %get-tuple-element.7.vortex_edge, f32[16,32,1024]{2,1,0:T(8,128)} %vortex.3, f32[32,1024]{1,0:T(8,128)} %wind.1, ...), custom_call_target="tpu_custom_call" | custom-call | tf_op jit(solution)/shard_map/backward/pallas_call | solution.py:349

commit v2 on v1

--- a/solution.py
+++ b/solution.py
@@ -14,6 +14,7 @@
 beta_plane = 1.0
 bottom_drag = 0.2
 MESH = pl.DeviceIdType.MESH
+ANY = pl.BlockSpec(memory_space=pl.ANY)
 VMEM = pl.BlockSpec(memory_space=pltpu.VMEM)
 SMEM = pl.BlockSpec(memory_space=pltpu.SMEM)
 
@@ -97,8 +98,9 @@
 
 
 def forward_kernel(
-    sizes, vortex, to_mode, radii, eigen, sine_high, sine_low,
-    field, carried, vortex_edge,
+    sizes, vortex_in, to_mode, radii, eigen, sine_high_in, sine_low_in,
+    field_out, carried, vortex_edge,
+    vortex, sine_high, sine_low, field, high, low, local,
     edge, moments, gathered, solved, landed, edge_landed,
     send_a, recv_a, send_b, recv_b, send_e, recv_e,
 ):
@@ -110,6 +112,13 @@
     def place(index):
         return (index // tiles, index % tiles)
 
+    loads = [
+        pltpu.make_async_copy(vortex_in, vortex, local.at[0]),
+        pltpu.make_async_copy(sine_high_in, sine_high, local.at[1]),
+        pltpu.make_async_copy(sine_low_in, sine_low, local.at[2]),
+    ]
+    for load in loads:
+        load.start()
     barrier = pltpu.get_barrier_semaphore()
 
     @pl.loop(1, count)
@@ -117,10 +126,6 @@
         pl.semaphore_signal(
             barrier, inc=1, device_id=place((me + step) % count), device_id_type=MESH
         )
-
-    edge[0] = vortex[:, rows - 1, :]
-    edge[1] = vortex[:, 0, :]
-    pl.semaphore_wait(barrier, count - 1)
 
     def edge_copy(side):
         target = (me + 1) % count if side == 0 else (me + count - 1) % count
@@ -130,30 +135,19 @@
             device_id=place(target), device_id_type=MESH,
         )
 
-    edge_copy(0).start()
-    edge_copy(1).start()
-
     chunk = min(rows, 16)
     mixer = spread_matrix(to_mode[...], chunk, True)
     shift = radius_column(radii, layers) + eigen[...]
     rho, _, _ = roots(shift)
+    loads[0].wait()
+    edge[0] = vortex[:, rows - 1, :]
+    edge[1] = vortex[:, 0, :]
     for part in range(rows // chunk):
         block = vortex[:, part * chunk : (part + 1) * chunk, :].reshape(layers * chunk, width)
-        modal = halves(dot3(mixer, halves(block)))
-        spectrum = dot3(modal, (sine_high[...], sine_low[...]))
-        field[part * chunk : (part + 1) * chunk] = spectrum.reshape(chunk, layers, width)
-
-    ahead = field[0]
-    for y in range(1, rows):
-        ahead = ahead * rho + field[y]
-    behind = field[rows - 1] * rho
-    for y in range(rows - 2, -1, -1):
-        behind = (behind + field[y]) * rho
-    for mode in range(layers):
-        for part in range(per_mode):
-            span = slice(part * piece, (part + 1) * piece)
-            moments[mode * per_mode + part, 0:1, :] = ahead[mode : mode + 1, span]
-            moments[mode * per_mode + part, 1:2, :] = behind[mode : mode + 1, span]
+        span = slice(part * chunk * layers, (part + 1) * chunk * layers)
+        high[span, :], low[span, :] = halves(dot3(mixer, halves(block)))
+    loads[1].wait()
+    loads[2].wait()
 
     def exchange(source, target, send, recv, step):
         other = (me + step) % count
@@ -163,10 +157,36 @@
             device_id=place(other), device_id_type=MESH,
         )
 
-    @pl.loop(1, count)
-    def _(step):
-        exchange(moments, gathered, send_a, recv_a, step).start()
-
+    for part in range(per_mode):
+        span = slice(part * piece, (part + 1) * piece)
+        spectrum = dot3((high[...], low[...]), (sine_high[:, span], sine_low[:, span]))
+        field[:, :, span] = spectrum.reshape(rows, layers, piece)
+        decay = rho[:, span]
+        ahead = field[0, :, span]
+        for y in range(1, rows):
+            ahead = ahead * decay + field[y, :, span]
+        behind = field[rows - 1, :, span] * decay
+        for y in range(rows - 2, -1, -1):
+            behind = (behind + field[y, :, span]) * decay
+        for mode in range(layers):
+            moments[mode * per_mode + part, 0:1, :] = ahead[mode : mode + 1]
+            moments[mode * per_mode + part, 1:2, :] = behind[mode : mode + 1]
+        if part == 0:
+            pl.semaphore_wait(barrier, count - 1)
+
+        @pl.loop(0, layers)
+        def _(turn):
+            other = (me // per_mode + turn) % layers * per_mode + part
+            step = (other - me + count) % count
+
+            @pl.when(step != 0)
+            def _():
+                exchange(moments, gathered, send_a, recv_a, step).start()
+
+    edge_copy(0).start()
+    edge_copy(1).start()
+    save = pltpu.make_async_copy(field, field_out, local.at[0])
+    save.start()
     gathered[me] = moments[me]
     mine = eigen[0:1, 0:piece]
     for part in range(1, per_mode):
@@ -221,16 +241,27 @@
         exchange(moments, gathered, send_a, recv_a, step).wait_send()
         exchange(solved, landed, send_b, recv_b, step).wait_send()
 
+    save.wait()
+
 
 def backward_kernel(
     sizes, field, carried, vortex_edge, vortex, wind, mask, to_layer, radii, eigen,
-    sine_high, sine_low,
-    fresh, stream,
-    high, low, stream_pad, vortex_pad, turn, cross,
+    sine_high_in, sine_low_in,
+    fresh_out, stream,
+    high, low, stream_pad, vortex_pad, turn, cross, cross_edge,
+    sine_high, sine_low, fresh, local, sent, saved,
 ):
     groups, tiles, layers, rows, width, piece = sizes
     count = groups * tiles
     me = lax.axis_index("group") * tiles + lax.axis_index("tile")
+    top = 8
+    loads = [
+        pltpu.make_async_copy(sine_high_in, sine_high, local.at[0]),
+        pltpu.make_async_copy(sine_low_in, sine_low, local.at[1]),
+        pltpu.make_async_copy(vortex, vortex_pad.at[:, pl.ds(top, rows), :], local.at[2]),
+    ]
+    for load in loads:
+        load.start()
     shift = radius_column(radii, layers) + eigen[...]
     rho, inverse, spread = roots(shift)
     factor = -0.5 / spread
@@ -252,26 +283,28 @@
     keep(rows, jnp.where(me == 0, 0.0, carried[0] + behind))
 
     chunk = min(rows, 16)
-    top = 8
+    loads[0].wait()
+    loads[1].wait()
     sine = (sine_high[...], sine_low[...])
     mixer = spread_matrix(to_layer[...], chunk, False)
+
+    def store(part):
+        return pltpu.make_async_copy(
+            stream_pad.at[:, pl.ds(top + part * chunk, chunk), :],
+            stream.at[:, pl.ds(part * chunk, chunk), :],
+            sent.at[part],
+        )
+
     for part in range(rows // chunk):
         span = slice(part * chunk * layers, (part + 1) * chunk * layers)
         modes = dot3((high[span, :], low[span, :]), sine)
         mixed = dot3(mixer, halves(modes)).reshape(layers, chunk, width)
-        stream[:, part * chunk : (part + 1) * chunk, :] = mixed
         stream_pad[:, top + part * chunk : top + (part + 1) * chunk, :] = mixed
+        store(part).start()
     span = slice(rows * layers, (rows + 2) * layers)
     modes = dot3((high[span, :], low[span, :]), sine)
     plain = halves(to_layer[...])
-    stream_pad[:, top - 1, :] = dot3(plain, halves(modes[:layers]))
-    stream_pad[:, top + rows, :] = dot3(plain, halves(modes[layers:]))
-    vortex_pad[:, top : top + rows, :] = vortex[...]
-    vortex_pad[:, top - 1, :] = vortex_edge[0]
-    vortex_pad[:, top + rows, :] = vortex_edge[1]
-
-    deep = rows + 2 * top
-    lane = lax.broadcasted_iota(jnp.int32, (deep, width), 1)
+    lane = lax.broadcasted_iota(jnp.int32, (max(rows, layers), width), 1)
 
     def east_west(value):
         lanes = lane[: value.shape[0]]
@@ -279,37 +312,59 @@
         west = jnp.where(lanes == 0, 0.0, pltpu.roll(value, 1, 1))
         return east, west
 
+    for side, row in ((0, top - 1), (1, top + rows)):
+        s_edge = dot3(plain, halves(modes[side * layers : (side + 1) * layers]))
+        q_edge = vortex_edge[side]
+        s_east, s_west = east_west(s_edge)
+        q_east, q_west = east_west(q_edge)
+        cross_edge[side] = q_edge * (s_east - s_west) - s_edge * (q_east - q_west)
+        stream_pad[:, row, :] = s_edge
+        vortex_pad[:, row, :] = q_edge
+    loads[2].wait()
+
     middle = slice(top, top + rows)
     north = slice(top + 1, top + rows + 1)
     south = slice(top - 1, top + rows - 1)
+
+    def finish(layer):
+        return pltpu.make_async_copy(fresh.at[layer], fresh_out.at[layer], saved.at[layer])
+
     damp = mask[...].astype(jnp.float32) * time_step
 
     @pl.loop(0, layers)
     def _(layer):
-        s_all = stream_pad[layer]
-        q_all = vortex_pad[layer]
-        s_east, s_west = east_west(s_all)
-        q_east, q_west = east_west(q_all)
+        s_mid = stream_pad[layer, middle, :]
+        q_mid = vortex_pad[layer, middle, :]
+        s_east, s_west = east_west(s_mid)
+        q_east, q_west = east_west(q_mid)
         s_across = s_east - s_west
         q_across = q_east - q_west
-        cross[...] = q_all * s_across - s_all * q_across
-        s_mid, q_mid = s_all[middle], q_all[middle]
+        cross[middle, :] = q_mid * s_across - s_mid * q_across
+        cross[top - 1 : top, :] = cross_edge[0, pl.ds(layer, 1), :]
+        cross[top + rows : top + rows + 1, :] = cross_edge[1, pl.ds(layer, 1), :]
         s_north, s_south = stream_pad[layer, north, :], stream_pad[layer, south, :]
         s_up = s_north - s_south
         q_up = vortex_pad[layer, north, :] - vortex_pad[layer, south, :]
         p_east, p_west = east_west(s_mid * q_up - q_mid * s_up)
-        across = s_across[middle]
         jacobian = (
-            across * q_up
-            - s_up * q_across[middle]
+            s_across * q_up
+            - s_up * q_across
             + (p_east - p_west)
             + (cross[north, :] - cross[south, :])
         ) * (1.0 / 12.0)
-        tendency = -jacobian - (beta_plane * 0.5) * across
+        tendency = -jacobian - (beta_plane * 0.5) * s_across
         forcing = jnp.where(layer == 0, wind[...], 0.0)
-        laplace = s_north + s_south + s_east[middle] + s_west[middle] - 4.0 * s_mid
+        laplace = s_north + s_south + s_east + s_west - 4.0 * s_mid
         drag = jnp.where(layer == layers - 1, bottom_drag, 0.0)
         fresh[layer] = q_mid + damp * (tendency + forcing - drag * laplace)
+        finish(layer).start()
+
+    @pl.loop(0, layers)
+    def _(layer):
+        finish(layer).wait()
+
+    for part in range(rows // chunk):
+        store(part).wait()
 
 
 def body(groups, tiles, vorticity, layer_to_mode, mode_to_layer, inverse_radii, wind, mask):
@@ -329,9 +384,16 @@
             jax.ShapeDtypeStruct((2, layers, width), f32),
             jax.ShapeDtypeStruct((2, layers, width), f32),
         ),
-        in_specs=[VMEM, VMEM, SMEM, VMEM, VMEM, VMEM],
-        out_specs=(VMEM, VMEM, VMEM),
+        in_specs=[ANY, VMEM, SMEM, VMEM, ANY, ANY],
+        out_specs=(ANY, VMEM, VMEM),
         scratch_shapes=[
+            pltpu.VMEM((layers, rows, width), f32),
+            pltpu.VMEM((width, width), bf16),
+            pltpu.VMEM((width, width), bf16),
+            pltpu.VMEM((rows, layers, width), f32),
+            pltpu.VMEM((rows * layers, width), bf16),
+            pltpu.VMEM((rows * layers, width), bf16),
+            dma((3,)),
             pltpu.VMEM((2, layers, width), f32),
             pltpu.VMEM((count, 2, piece), f32),
             pltpu.VMEM((count, 2, piece), f32),
@@ -352,8 +414,8 @@
             jax.ShapeDtypeStruct((layers, rows, width), f32),
             jax.ShapeDtypeStruct((layers, rows, width), f32),
         ),
-        in_specs=[VMEM] * 7 + [SMEM] + [VMEM] * 3,
-        out_specs=(VMEM, VMEM),
+        in_specs=[VMEM] * 3 + [ANY] + [VMEM] * 3 + [SMEM, VMEM, ANY, ANY],
+        out_specs=(ANY, ANY),
         scratch_shapes=[
             pltpu.VMEM((total, width), bf16),
             pltpu.VMEM((total, width), bf16),
@@ -361,6 +423,11 @@
             pltpu.VMEM((layers, rows + 16, width), f32),
             pltpu.VMEM((rows, layers, width), f32),
             pltpu.VMEM((rows + 16, width), f32),
+            pltpu.VMEM((2, layers, width), f32),
+            pltpu.VMEM((width, width), bf16),
+            pltpu.VMEM((width, width), bf16),
+            pltpu.VMEM((layers, rows, width), f32),
+            dma((3,)), dma((rows // min(rows, 16),)), dma((layers,)),
         ],
         compiler_params=pltpu.CompilerParams(vmem_limit_bytes=limit),
         name="backward",

time: 47 us -> 39.1 us (0.83)
  Pallas kernels: 46.3 us -> 38.3 us
    pallas_call x1, Pallas kernels: 28.4 us -> 22 us  [body(): pl.pallas_call(functools.partial(forward_kernel, sizes), out_shape=(jax.S...]
    pallas_call x1, Pallas kernels: 17.9 us -> 16.3 us  [body(): pl.pallas_call(functools.partial(backward_kernel, sizes), out_shape=(jax....]
where the time goes in v2:
time: 39.1 us; the launch traced here: 38.9 us
  Pallas kernels  38.3 us (98%)
  between operations  0.64 us (2%)
    pallas_call x1, Pallas kernels, body(): pl.pallas_call(functools.partial(forward_kernel, sizes), out_shape=(jax.S...  22 us
    pallas_call x1, Pallas kernels, body(): pl.pallas_call(functools.partial(backward_kernel, sizes), out_shape=(jax....  16.3 us

profile of v2, /device:TPU:0, one launch (start us, length us, event | category | flops | bytes accessed | tf_op | source)
XLA Modules:
  0.0 38.9 jit_solution(13362206675507616801)
XLA Ops:
  0.6 22.0 %forward.1 = (f32[32,16,1024]{2,1,0:T(8,128)}, f32[2,16,1024]{2,1,0:T(8,128)}, f32[2,16,1024]{2,1,0:T(8,128)}) custom-call(f32[16,32,1024]{2,1,0:T(8,128)} %vortex.1, f32[16,16]{1,0:T(8,128)} %to_mode.1, f32[16]{0:T(128)} %radii.3, f32[1,1024]{1,0:T(1,128)} %constant.8.clone.eigen, bf16[1024,1024]{1,0:T(8,128)(2,1)} %constant.6.clone.sine_high_in, ...), custom_call_target="tpu_custom_call" | custom-call | tf_op jit(solution)/shard_map/forward/pallas_call | solution.py:380
  22.6 16.3 %backward.1 = (f32[16,32,1024]{2,1,0:T(8,128)}, f32[16,32,1024]{2,1,0:T(8,128)}) custom-call(f32[32,16,1024]{2,1,0:T(8,128)} %get-tuple-element.5.field, f32[2,16,1024]{2,1,0:T(8,128)} %get-tuple-element.6.carried, f32[2,16,1024]{2,1,0:T(8,128)} %get-tuple-element.7.vortex_edge, f32[16,32,1024]{2,1,0:T(8,128)} %vortex.1, f32[32,1024]{1,0:T(8,128)} %wind.1, ...), custom_call_target="tpu_custom_call" | custom-call | tf_op jit(solution)/shard_map/backward/pallas_call | solution.py:411

commit v3 on v2

--- a/solution.py
+++ b/solution.py
@@ -110,7 +110,10 @@
     me = lax.axis_index("group") * tiles + lax.axis_index("tile")
 
     def place(index):
-        return (index // tiles, index % tiles)
+        return (lax.div(index, tiles), lax.rem(index, tiles))
+
+    def wrap(index):
+        return jnp.where(index >= count, index - count, index)
 
     loads = [
         pltpu.make_async_copy(vortex_in, vortex, local.at[0]),
@@ -124,7 +127,7 @@
     @pl.loop(1, count)
     def _(step):
         pl.semaphore_signal(
-            barrier, inc=1, device_id=place((me + step) % count), device_id_type=MESH
+            barrier, inc=1, device_id=place(wrap(me + step)), device_id_type=MESH
         )
 
     def edge_copy(side):
@@ -150,13 +153,14 @@
     loads[2].wait()
 
     def exchange(source, target, send, recv, step):
-        other = (me + step) % count
+        other = wrap(me + step)
         return pltpu.make_async_remote_copy(
             src_ref=source.at[other], dst_ref=target.at[me],
             send_sem=send.at[step], recv_sem=recv.at[step],
             device_id=place(other), device_id_type=MESH,
         )
 
+    home = lax.div(me, per_mode)
     for part in range(per_mode):
         span = slice(part * piece, (part + 1) * piece)
         spectrum = dot3((high[...], low[...]), (sine_high[:, span], sine_low[:, span]))
@@ -176,8 +180,8 @@
 
         @pl.loop(0, layers)
         def _(turn):
-            other = (me // per_mode + turn) % layers * per_mode + part
-            step = (other - me + count) % count
+            other = lax.rem(home + turn, layers) * per_mode + part
+            step = wrap(other - me + count)
 
             @pl.when(step != 0)
             def _():
@@ -249,7 +253,7 @@
     sine_high_in, sine_low_in,
     fresh_out, stream,
     high, low, stream_pad, vortex_pad, turn, cross, cross_edge,
-    sine_high, sine_low, fresh, local, sent, saved,
+    sine_high, sine_low, fresh, partial, damp, local, sent, saved,
 ):
     groups, tiles, layers, rows, width, piece = sizes
     count = groups * tiles
@@ -322,41 +326,53 @@
         vortex_pad[:, row, :] = q_edge
     loads[2].wait()
 
-    middle = slice(top, top + rows)
-    north = slice(top + 1, top + rows + 1)
-    south = slice(top - 1, top + rows - 1)
-
     def finish(layer):
         return pltpu.make_async_copy(fresh.at[layer], fresh_out.at[layer], saved.at[layer])
 
-    damp = mask[...].astype(jnp.float32) * time_step
+    damp[...] = mask[...].astype(jnp.float32) * time_step
+
+    block = 8
 
     @pl.loop(0, layers)
     def _(layer):
-        s_mid = stream_pad[layer, middle, :]
-        q_mid = vortex_pad[layer, middle, :]
-        s_east, s_west = east_west(s_mid)
-        q_east, q_west = east_west(q_mid)
-        s_across = s_east - s_west
-        q_across = q_east - q_west
-        cross[middle, :] = q_mid * s_across - s_mid * q_across
         cross[top - 1 : top, :] = cross_edge[0, pl.ds(layer, 1), :]
         cross[top + rows : top + rows + 1, :] = cross_edge[1, pl.ds(layer, 1), :]
-        s_north, s_south = stream_pad[layer, north, :], stream_pad[layer, south, :]
-        s_up = s_north - s_south
-        q_up = vortex_pad[layer, north, :] - vortex_pad[layer, south, :]
-        p_east, p_west = east_west(s_mid * q_up - q_mid * s_up)
-        jacobian = (
-            s_across * q_up
-            - s_up * q_across
-            + (p_east - p_west)
-            + (cross[north, :] - cross[south, :])
-        ) * (1.0 / 12.0)
-        tendency = -jacobian - (beta_plane * 0.5) * s_across
-        forcing = jnp.where(layer == 0, wind[...], 0.0)
-        laplace = s_north + s_south + s_east + s_west - 4.0 * s_mid
-        drag = jnp.where(layer == layers - 1, bottom_drag, 0.0)
-        fresh[layer] = q_mid + damp * (tendency + forcing - drag * laplace)
+        for start in range(top, top + rows, block):
+            here = slice(start, start + block)
+            north, south = slice(start + 1, start + block + 1), slice(start - 1, start + block - 1)
+            s_mid, q_mid = stream_pad[layer, here, :], vortex_pad[layer, here, :]
+            s_east, s_west = east_west(s_mid)
+            q_east, q_west = east_west(q_mid)
+            s_across = s_east - s_west
+            q_across = q_east - q_west
+            cross[here, :] = q_mid * s_across - s_mid * q_across
+            s_up = stream_pad[layer, north, :] - stream_pad[layer, south, :]
+            q_up = vortex_pad[layer, north, :] - vortex_pad[layer, south, :]
+            p_east, p_west = east_west(s_mid * q_up - q_mid * s_up)
+            partial[start - top : start - top + block, :] = (
+                (s_across * q_up - s_up * q_across + (p_east - p_west)) * (1.0 / 12.0)
+                + (beta_plane * 0.5) * s_across
+            )
+        for start in range(top, top + rows, block):
+            here = slice(start, start + block)
+            north, south = slice(start + 1, start + block + 1), slice(start - 1, start + block - 1)
+            out = slice(start - top, start - top + block)
+            loss = partial[out, :] + (cross[north, :] - cross[south, :]) * (1.0 / 12.0)
+            fresh[layer, out, :] = vortex_pad[layer, here, :] - damp[out, :] * loss
+
+        @pl.when(layer == 0)
+        def _():
+            fresh[layer] = fresh[layer] + damp[...] * wind[...]
+
+        @pl.when(layer == layers - 1)
+        def _():
+            s_mid = stream_pad[layer, top : top + rows, :]
+            s_east, s_west = east_west(s_mid)
+            s_north = stream_pad[layer, top + 1 : top + rows + 1, :]
+            s_south = stream_pad[layer, top - 1 : top + rows - 1, :]
+            laplace = s_north + s_south + s_east + s_west - 4.0 * s_mid
+            fresh[layer] = fresh[layer] - (bottom_drag * damp[...]) * laplace
+
         finish(layer).start()
 
     @pl.loop(0, layers)
@@ -427,6 +443,8 @@
             pltpu.VMEM((width, width), bf16),
             pltpu.VMEM((width, width), bf16),
             pltpu.VMEM((layers, rows, width), f32),
+            pltpu.VMEM((rows, width), f32),
+            pltpu.VMEM((rows, width), f32),
             dma((3,)), dma((rows // min(rows, 16),)), dma((layers,)),
         ],
         compiler_params=pltpu.CompilerParams(vmem_limit_bytes=limit),

time: 39.1 us -> 38.6 us (0.987)
  Pallas kernels: 38.3 us -> 37.7 us
where the time goes in v3:
time: 38.6 us; the launch traced here: 38.4 us
  Pallas kernels  37.7 us (98%)
  between operations  0.64 us (2%)
    pallas_call x1, Pallas kernels, body(): pl.pallas_call(functools.partial(forward_kernel, sizes), out_shape=(jax.S...  21.6 us
    pallas_call x1, Pallas kernels, body(): pl.pallas_call(functools.partial(backward_kernel, sizes), out_shape=(jax....  16.1 us

profile of v3, /device:TPU:0, one launch (start us, length us, event | category | flops | bytes accessed | tf_op | source)
XLA Modules:
  0.0 38.4 jit_solution(7942238300950908066)
XLA Ops:
  0.6 21.6 %forward.1 = (f32[32,16,1024]{2,1,0:T(8,128)}, f32[2,16,1024]{2,1,0:T(8,128)}, f32[2,16,1024]{2,1,0:T(8,128)}) custom-call(f32[16,32,1024]{2,1,0:T(8,128)} %vortex.1, f32[16,16]{1,0:T(8,128)} %to_mode.1, f32[16]{0:T(128)} %radii.3, f32[1,1024]{1,0:T(1,128)} %constant.8.clone.eigen, bf16[1024,1024]{1,0:T(8,128)(2,1)} %constant.6.clone.sine_high_in, ...), custom_call_target="tpu_custom_call" | custom-call | tf_op jit(solution)/shard_map/forward/pallas_call | solution.py:396
  22.2 16.1 %backward.1 = (f32[16,32,1024]{2,1,0:T(8,128)}, f32[16,32,1024]{2,1,0:T(8,128)}) custom-call(f32[32,16,1024]{2,1,0:T(8,128)} %get-tuple-element.5.field, f32[2,16,1024]{2,1,0:T(8,128)} %get-tuple-element.6.carried, f32[2,16,1024]{2,1,0:T(8,128)} %get-tuple-element.7.vortex_edge, f32[16,32,1024]{2,1,0:T(8,128)} %vortex.1, f32[32,1024]{1,0:T(8,128)} %wind.1, ...), custom_call_target="tpu_custom_call" | custom-call | tf_op jit(solution)/shard_map/backward/pallas_call | solution.py:427

commit v4 on v3

--- a/solution.py
+++ b/solution.py
@@ -44,8 +44,10 @@
 
 
 def dot3(left, right):
-    (left_high, left_low), (right_high, right_low) = left, right
-    return dot(left_high, right_high) + (dot(left_low, right_high) + dot(left_high, right_low))
+    right_high, right_low = right
+    rows = left.shape[0] // 2
+    wide = dot(left, right_high)
+    return wide[:rows] + (wide[rows:] + dot(left[:rows], right_low))
 
 
 def power(base, exponent):
@@ -94,13 +96,13 @@
     for part in halves(matrix):
         full = dot(dot(left, part).astype(jnp.bfloat16), right)
         parts.append(jnp.where(same, full, 0.0).astype(jnp.bfloat16))
-    return tuple(parts)
+    return jnp.concatenate(parts, axis=0)
 
 
 def forward_kernel(
     sizes, vortex_in, to_mode, radii, eigen, sine_high_in, sine_low_in,
     field_out, carried, vortex_edge,
-    vortex, sine_high, sine_low, field, high, low, local,
+    vortex, sine_high, sine_low, field, both, local,
     edge, moments, gathered, solved, landed, edge_landed,
     send_a, recv_a, send_b, recv_b, send_e, recv_e,
 ):
@@ -147,8 +149,10 @@
     edge[1] = vortex[:, 0, :]
     for part in range(rows // chunk):
         block = vortex[:, part * chunk : (part + 1) * chunk, :].reshape(layers * chunk, width)
+        low_at = rows * layers
         span = slice(part * chunk * layers, (part + 1) * chunk * layers)
-        high[span, :], low[span, :] = halves(dot3(mixer, halves(block)))
+        low_span = slice(low_at + part * chunk * layers, low_at + (part + 1) * chunk * layers)
+        both[span, :], both[low_span, :] = halves(dot3(mixer, halves(block)))
     loads[1].wait()
     loads[2].wait()
 
@@ -163,7 +167,7 @@
     home = lax.div(me, per_mode)
     for part in range(per_mode):
         span = slice(part * piece, (part + 1) * piece)
-        spectrum = dot3((high[...], low[...]), (sine_high[:, span], sine_low[:, span]))
+        spectrum = dot3(both[...], (sine_high[:, span], sine_low[:, span]))
         field[:, :, span] = spectrum.reshape(rows, layers, piece)
         decay = rho[:, span]
         ahead = field[0, :, span]
@@ -252,7 +256,7 @@
     sizes, field, carried, vortex_edge, vortex, wind, mask, to_layer, radii, eigen,
     sine_high_in, sine_low_in,
     fresh_out, stream,
-    high, low, stream_pad, vortex_pad, turn, cross, cross_edge,
+    both, stream_pad, vortex_pad, turn, cross, cross_edge,
     sine_high, sine_low, fresh, partial, damp, local, sent, saved,
 ):
     groups, tiles, layers, rows, width, piece = sizes
@@ -272,8 +276,9 @@
 
     def keep(slot, value):
         upper, lower = halves(value * factor)
-        high[slot * layers : (slot + 1) * layers, :] = upper
-        low[slot * layers : (slot + 1) * layers, :] = lower
+        both[slot * layers : (slot + 1) * layers, :] = upper
+        slot = slot + rows + 2
+        both[slot * layers : (slot + 1) * layers, :] = lower
 
     ahead = carried[0]
     for y in range(rows):
@@ -299,15 +304,14 @@
             sent.at[part],
         )
 
+    modes = dot3(both[...], sine)
     for part in range(rows // chunk):
         span = slice(part * chunk * layers, (part + 1) * chunk * layers)
-        modes = dot3((high[span, :], low[span, :]), sine)
-        mixed = dot3(mixer, halves(modes)).reshape(layers, chunk, width)
+        mixed = dot3(mixer, halves(modes[span])).reshape(layers, chunk, width)
         stream_pad[:, top + part * chunk : top + (part + 1) * chunk, :] = mixed
         store(part).start()
-    span = slice(rows * layers, (rows + 2) * layers)
-    modes = dot3((high[span, :], low[span, :]), sine)
-    plain = halves(to_layer[...])
+    outer = modes[rows * layers :]
+    plain = jnp.concatenate(halves(to_layer[...]), axis=0)
     lane = lax.broadcasted_iota(jnp.int32, (max(rows, layers), width), 1)
 
     def east_west(value):
@@ -317,7 +321,7 @@
         return east, west
 
     for side, row in ((0, top - 1), (1, top + rows)):
-        s_edge = dot3(plain, halves(modes[side * layers : (side + 1) * layers]))
+        s_edge = dot3(plain, halves(outer[side * layers : (side + 1) * layers]))
         q_edge = vortex_edge[side]
         s_east, s_west = east_west(s_edge)
         q_east, q_west = east_west(q_edge)
@@ -407,8 +411,7 @@
             pltpu.VMEM((width, width), bf16),
             pltpu.VMEM((width, width), bf16),
             pltpu.VMEM((rows, layers, width), f32),
-            pltpu.VMEM((rows * layers, width), bf16),
-            pltpu.VMEM((rows * layers, width), bf16),
+            pltpu.VMEM((2 * rows * layers, width), bf16),
             dma((3,)),
             pltpu.VMEM((2, layers, width), f32),
             pltpu.VMEM((count, 2, piece), f32),
@@ -433,8 +436,7 @@
         in_specs=[VMEM] * 3 + [ANY] + [VMEM] * 3 + [SMEM, VMEM, ANY, ANY],
         out_specs=(ANY, ANY),
         scratch_shapes=[
-            pltpu.VMEM((total, width), bf16),
-            pltpu.VMEM((total, width), bf16),
+            pltpu.VMEM((2 * total, width), bf16),
             pltpu.VMEM((layers, rows + 16, width), f32),
             pltpu.VMEM((layers, rows + 16, width), f32),
             pltpu.VMEM((rows, layers, width), f32),

time: 38.6 us -> 37.5 us (0.972)
  Pallas kernels: 37.7 us -> 36.7 us
    pallas_call x1, Pallas kernels: 16.1 us -> 15.1 us  [body(): pl.pallas_call(functools.partial(backward_kernel, sizes), out_shape=(jax....]
where the time goes in v4:
time: 37.5 us; the launch traced here: 37.3 us
  Pallas kernels  36.7 us (98%)
  between operations  0.64 us (2%)
    pallas_call x1, Pallas kernels, body(): pl.pallas_call(functools.partial(forward_kernel, sizes), out_shape=(jax.S...  21.6 us
    pallas_call x1, Pallas kernels, body(): pl.pallas_call(functools.partial(backward_kernel, sizes), out_shape=(jax....  15.1 us

profile of v4, /device:TPU:0, one launch (start us, length us, event | category | flops | bytes accessed | tf_op | source)
XLA Modules:
  0.0 37.3 jit_solution(7205641550753753656)
XLA Ops:
  0.6 21.6 %forward.1 = (f32[32,16,1024]{2,1,0:T(8,128)}, f32[2,16,1024]{2,1,0:T(8,128)}, f32[2,16,1024]{2,1,0:T(8,128)}) custom-call(f32[16,32,1024]{2,1,0:T(8,128)} %vortex.1, f32[16,16]{1,0:T(8,128)} %to_mode.1, f32[16]{0:T(128)} %radii.3, f32[1,1024]{1,0:T(1,128)} %constant.8.clone.eigen, bf16[1024,1024]{1,0:T(8,128)(2,1)} %constant.6.clone.sine_high_in, ...), custom_call_target="tpu_custom_call" | custom-call | tf_op jit(solution)/shard_map/forward/pallas_call | solution.py:400
  22.2 15.1 %backward.1 = (f32[16,32,1024]{2,1,0:T(8,128)}, f32[16,32,1024]{2,1,0:T(8,128)}) custom-call(f32[32,16,1024]{2,1,0:T(8,128)} %get-tuple-element.5.field, f32[2,16,1024]{2,1,0:T(8,128)} %get-tuple-element.6.carried, f32[2,16,1024]{2,1,0:T(8,128)} %get-tuple-element.7.vortex_edge, f32[16,32,1024]{2,1,0:T(8,128)} %vortex.1, f32[32,1024]{1,0:T(8,128)} %wind.1, ...), custom_call_target="tpu_custom_call" | custom-call | tf_op jit(solution)/shard_map/backward/pallas_call | solution.py:430
